TPU v7x, 512 devices: a whole 4x4x16 slice. The times are simulated.
512 devices in a mesh: island: 64 (over y, x, z_hi, core), fsdp: 8 (over z_lo).
Axes of the slice: x: 4, y: 4, z: 16 (z_hi: 2, z_lo: 8; z = z_hi * 8 + z_lo), core: 2. Of those that a mesh axis runs over, the one named last changes fastest.
Arguments:
- anchor: float32 [8192, 128], P('fsdp'), may hold values from -6 to 6
- inner_drift: float32 [64, 8192, 128], P('island', 'fsdp'), may hold values from -6 to 6
- gradient: bfloat16 [64, 8192, 128], P('island', 'fsdp'), may hold values from -400 to 400
- first_moment: float32 [64, 8192, 128], P('island', 'fsdp'), may hold values from -6 to 6
- second_moment: float32 [64, 8192, 128], P('island', 'fsdp'), may hold values from 0.1 to 4
- outer_momentum: float32 [8192, 128], P('fsdp'), may hold values from -6 to 6
Outputs:
- new_first: float32 [64, 8192, 128], P('island', 'fsdp')
- new_second: float32 [64, 8192, 128], P('island', 'fsdp')
- new_anchor: float32 [8192, 128], P('fsdp')
- new_momentum: float32 [8192, 128], P('fsdp')
All inputs are finite; a program needn't handle non-finite values.
Results may differ from a plain program's by a relative error of at most 0.0003.
Values sent between devices are 32-bit elements; how exact they have to be, the bound alone decides.
A program may use at most 64 MiB of HBM per device.

v0:
```python
import math

import jax
import jax.numpy as jnp
from jax import lax
from jax.sharding import PartitionSpec as P

INNER_STEP = 500


BETA_ONE = 0.9
BETA_TWO = 0.95
adam_epsilon = 1e-08
inner_rate = 0.3
decay_rate = 0.1
outer_rate = 0.7
outer_beta = 0.9


def adam_rows(anchor, drift, gradient, first, second, factor):
    params = anchor + drift
    clipped = gradient.astype(jnp.float32) * factor
    new_first = BETA_ONE * first + (1.0 - BETA_ONE) * clipped
    new_second = BETA_TWO * second + (1.0 - BETA_TWO) * clipped * clipped
    first_fix = 1.0 - BETA_ONE**INNER_STEP
    second_fix = 1.0 - BETA_TWO**INNER_STEP
    adam = new_first / first_fix / (jnp.sqrt(new_second / second_fix) + adam_epsilon)
    updated = params - inner_rate * (adam + decay_rate * params)
    return (new_first, new_second, anchor - updated)


def outer_update(anchor, momentum, summed, count):
    average = summed / count
    new_momentum = outer_beta * momentum + average
    new_anchor = anchor - outer_rate * (average + outer_beta * new_momentum)
    return (new_anchor, new_momentum)


def per_device(anchor, inner_drift, gradient, first_moment, second_moment, outer_momentum):
    drift = inner_drift[0]
    grads = gradient[0]
    first = first_moment[0]
    second = second_moment[0]
    rows, lanes = anchor.shape
    limit = math.sqrt(lax.axis_size("fsdp") * rows * lanes)
    wide = grads.astype(jnp.float32)
    squares = lax.psum(jnp.sum(wide * wide), "fsdp")
    factor = jnp.minimum(1.0, limit / (jnp.sqrt(squares) + 1e-06))
    islands = float(lax.axis_size("island"))
    new_first, new_second, pseudo = adam_rows(anchor, drift, grads, first, second, factor)
    summed = lax.psum(pseudo, "island")
    new_anchor, new_momentum = outer_update(anchor, outer_momentum, summed, islands)
    return (new_first[None], new_second[None], new_anchor, new_momentum)


def solution(mesh):
    return jax.shard_map(
        per_device,
        mesh=mesh,
        in_specs=(
            P("fsdp", None),
            P("island", "fsdp", None),
            P("island", "fsdp", None),
            P("island", "fsdp", None),
            P("island", "fsdp", None),
            P("fsdp", None),
        ),
        out_specs=(
            P("island", "fsdp", None),
            P("island", "fsdp", None),
            P("fsdp", None),
            P("fsdp", None),
        ),
        check_vma=False,
    )
```

profile of v0, /device:TPU:1, one launch (start us, length us, event | category | flops | bytes accessed | tf_op | source)
XLA Modules:
  0.0 1129.5 jit_solution(9653909580910652458)
XLA Ops:
  7.2 0.0 copy-start
  7.2 0.0 all-reduce.2.cloned.1.call-start
  7.2 1.7 fusion.10
  8.9 34.0 %psum.14 = f32[]{:T(128)} all-reduce(f32[]{:T(128)} %fusion.10), channel_id=1, replica_groups=mesh['island'=64,'fsdp'=8] {'fsdp'}, use_global_device_ids=true, to_apply=%region_1.0 | all-reduce | flops 1 | bytes 8 | tf_op jit(solution)/shard_map/psum | solution.py:47
  43.6 0.0 copy-done
  43.6 0.0 copy-start.2
  43.7 2.8 fusion.8
  46.5 0.0 copy-start.1
  46.5 0.0 all-reduce.2.cloned.1.call-update
  46.5 0.0 copy-done.2
  46.5 1.0 copy-done.1
  47.5 0.0 copy-start.3
  47.5 0.0 copy-start.4
  47.5 1.1 fusion.11
  48.6 1071.9 %all-reduce.2.cloned.1.call-done = f32[1024,128]{1,0:T(8,128)} async-done(((f32[1024,128]{1,0:T(8,128)}), f32[1024,128]{1,0:T(8,128)}) %all-reduce.2.cloned.1.call-update) | async-done | bytes 524304 | tf_op jit(solution)/shard_map/psum | solution.py:51
  1120.5 0.0 copy-done.3
  1120.5 0.0 copy-done.4
  1120.5 2.1 multiply_subtract_fusion
Async XLA Ops:
  7.2 36.5 %copy-start = (bf16[1,1024,128]{2,1,0:T(8,128)(2,1)S(1)}, bf16[1,1024,128]{2,1,0:T(8,128)(2,1)}, u32[]{:S(2)}) copy-start(bf16[1,1024,128]{2,1,0:T(8,128)(2,1)} %param.8) | copy-start | bytes 786436
  7.2 1113.4 %all-reduce.2.cloned.1.call-start = ((), (), s32[]{:S(2)}) async-start(), calls=%async_computation | async-start | bytes 1048576 | tf_op jit(solution)/shard_map/psum | solution.py:51
  43.6 2.8 copy-start.2
  46.5 1.0 copy-start.1
  47.5 1073.0 %copy-start.3 = (f32[1024,128]{1,0:T(8,128)S(1)}, f32[1024,128]{1,0:T(8,128)}, u32[]{:S(2)}) copy-start(f32[1024,128]{1,0:T(8,128)} %param.6) | copy-start | bytes 1572868
  47.5 1073.0 %copy-start.4 = (f32[1024,128]{1,0:T(8,128)S(1)}, f32[1024,128]{1,0:T(8,128)}, u32[]{:S(2)}) copy-start(f32[1024,128]{1,0:T(8,128)} %param.11) | copy-start | bytes 1572868
Sparse Core Ops, SparseCore 0:
  46.6 1073.8 all-reduce.1
where the time goes:
time: 1130 us
  waiting for transfers between devices  1070 us (95%)
  blocking collectives  34 us (3%)
  between operations  14.8 us (1%)
    psum x1, waiting for transfers between devices, per_device(): summed = lax.psum(pseudo, 'island')  1070 us
    psum x1, blocking collectives, per_device(): squares = lax.psum(jnp.sum(wide * wide), 'fsdp')  34 us
  transfers between devices with their start and end apart: 1, of which 1 were waited for; matrix products, arithmetic and copies ran while one was open for 0% of the time, Pallas kernels for 0%

commit v1 on v0

v1 whole, which is shorter than its diff:
```python
import functools
import math

import jax
import jax.numpy as jnp
from jax import lax
from jax.experimental import pallas as pl
from jax.experimental.pallas import tpu as pltpu
from jax.sharding import PartitionSpec as P

INNER_STEP = 500
BETA_ONE = 0.9
BETA_TWO = 0.95
ADAM_EPSILON = 1e-08
INNER_RATE = 0.3
DECAY_RATE = 0.1
OUTER_RATE = 0.7
OUTER_BETA = 0.9

SIDE = 4
PLANE = SIDE * SIDE
MESH = pl.DeviceIdType.MESH


def adam_rows(anchor, drift, gradient, first, second, factor):
    params = anchor + drift
    clipped = gradient.astype(jnp.float32) * factor
    new_first = BETA_ONE * first + (1.0 - BETA_ONE) * clipped
    new_second = BETA_TWO * second + (1.0 - BETA_TWO) * clipped * clipped
    first_fix = 1.0 - BETA_ONE**INNER_STEP
    second_fix = 1.0 - BETA_TWO**INNER_STEP
    adam = new_first / first_fix / (jnp.sqrt(new_second / second_fix) + ADAM_EPSILON)
    updated = params - INNER_RATE * (adam + DECAY_RATE * params)
    return (new_first, new_second, anchor - updated)


def outer_update(anchor, momentum, summed, count):
    average = summed / count
    new_momentum = OUTER_BETA * momentum + average
    new_anchor = anchor - OUTER_RATE * (average + OUTER_BETA * new_momentum)
    return (new_anchor, new_momentum)


def kernel(
    shards, islands, limit,
    anchor_hbm, drift_hbm, grad_hbm, first_hbm, second_hbm, mom_hbm,
    new_first, new_second, na, nm,
    anchor, drift, grad, first, second, mom,
    part, parts, sib_out, own, sib_in, plane_out, plane_in, z_out, z_in, full,
    in_sems, part_send, part_recv, sib_send, sib_recv,
    plane_send, plane_recv, z_send, z_recv, all_send, all_recv, fwd_send, fwd_recv,
):
    rows = anchor.shape[0]
    half = rows // 2
    step = half // PLANE
    island = lax.axis_index("island")
    shard = lax.axis_index("fsdp")
    core = island % 2
    far = (island // 2) % 2
    place = island // 4
    py, px = place // SIDE, place % SIDE

    def spot(r):
        return ((py + r // SIDE) % SIDE) * SIDE + (px + r % SIDE) % SIDE

    def back(r):
        return ((py + SIDE - r // SIDE) % SIDE) * SIDE + (px + SIDE - r % SIDE) % SIDE

    def peer(r):
        return (spot(r) * 4 + far * 2 + core, shard)

    sibling = (place * 4 + far * 2 + (1 - core), shard)
    across = (place * 4 + (1 - far) * 2 + core, shard)

    def mate(k):
        return (island, (shard + k) % shards)

    def span(c, p):
        return pl.ds(pl.multiple_of(c * half + p * step, step), step)

    loads = [
        pltpu.make_async_copy(src, dst, in_sems.at[i])
        for i, (src, dst) in enumerate(
            [(grad_hbm, grad), (first_hbm, first), (second_hbm, second),
             (anchor_hbm, anchor), (drift_hbm, drift), (mom_hbm, mom)])
    ]
    for load in loads:
        load.start()

    barrier = pltpu.get_barrier_semaphore()
    for k in range(1, shards):
        pl.semaphore_signal(barrier, inc=1, device_id=mate(k), device_id_type=MESH)
    pl.semaphore_signal(barrier, inc=1, device_id=across, device_id_type=MESH)
    pl.semaphore_signal(barrier, inc=1, device_id=sibling, device_id_type=MESH)
    for r in range(1, PLANE):
        pl.semaphore_signal(barrier, inc=1, device_id=peer(r), device_id_type=MESH)

    loads[0].wait()
    wide = grad[...].astype(jnp.float32)
    part[...] = jnp.sum((wide * wide).reshape(rows // 8, 8, 128), axis=0)
    pl.semaphore_wait(barrier, shards - 1 + 2 + PLANE - 1)

    def part_copy(k):
        return pltpu.make_async_remote_copy(
            part, parts.at[k], part_send.at[k], part_recv.at[k], device_id=mate(k), device_id_type=MESH)

    for k in range(1, shards):
        part_copy(k).start()
    for load in loads[1:]:
        load.wait()
    total = part[...]
    for k in range(1, shards):
        part_copy(k).wait_recv()
        total = total + parts[k]
    squares = jnp.sum(total)
    factor = jnp.minimum(1.0, limit / (jnp.sqrt(jnp.full((8, 128), squares, jnp.float32)) + 1e-06))
    factor = jnp.concatenate([factor] * (step // 8), axis=0)

    def adam_block(where):
        nf, ns, pseudo = adam_rows(
            anchor[where, :], drift[where, :], grad[where, :], first[where, :], second[where, :], factor)
        new_first[where, :] = nf
        new_second[where, :] = ns
        return pseudo

    def sib_copy(r):
        return pltpu.make_async_remote_copy(
            sib_out.at[r], sib_in.at[r], sib_send.at[r], sib_recv.at[r], device_id=sibling, device_id_type=MESH)

    @pl.loop(1, PLANE + 1)
    def _(i):
        r = i % PLANE
        sib_out[r] = adam_block(span(1 - core, spot(r)))
        sib_copy(r).start()

    @pl.loop(0, PLANE)
    def _(r):
        own[r] = adam_block(span(core, spot(r)))

    def plane_copy(r):
        return pltpu.make_async_remote_copy(
            plane_out.at[r], plane_in.at[r], plane_send.at[r], plane_recv.at[r],
            device_id=peer(r), device_id_type=MESH)

    @pl.loop(1, PLANE)
    def _(r):
        sib_copy(r).wait_recv()
        plane_out[r] = own[r] + sib_in[r]
        plane_copy(r).start()

    sib_copy(0).wait_recv()

    def add(r, acc):
        plane_copy(r).wait_recv()
        return acc + plane_in[r]

    z_out[...] = lax.fori_loop(1, PLANE, add, own[0] + sib_in[0])
    z_copy = pltpu.make_async_remote_copy(
        z_out, z_in, z_send, z_recv, device_id=across, device_id_type=MESH)
    z_copy.start()
    z_copy.wait_recv()
    mine = span(core, place)
    full[mine, :] = z_out[...] + z_in[...]

    def all_copy(r):
        return pltpu.make_async_remote_copy(
            full.at[mine, :], full.at[mine, :], all_send.at[r], all_recv.at[r],
            device_id=peer(r), device_id_type=MESH)

    def fwd_copy(r):
        where = span(core, back(r))
        return pltpu.make_async_remote_copy(
            full.at[where, :], full.at[where, :], fwd_send.at[r], fwd_recv.at[r],
            device_id=sibling, device_id_type=MESH)

    @pl.loop(1, PLANE)
    def _(r):
        all_copy(r).start()

    fwd_copy(0).start()

    def outer_block(where):
        na[where, :], nm[where, :] = outer_update(anchor[where, :], mom[where, :], full[where, :], islands)

    outer_block(mine)

    @pl.loop(1, PLANE)
    def _(r):
        where = span(core, back(r))
        pltpu.make_async_remote_copy(
            full.at[where, :], full.at[where, :], all_send.at[r], all_recv.at[r],
            device_id=peer(r), device_id_type=MESH).wait_recv()
        fwd_copy(r).start()
        outer_block(where)

    @pl.loop(0, PLANE)
    def _(r):
        where = span(1 - core, back(r))
        pltpu.make_async_remote_copy(
            full.at[where, :], full.at[where, :], fwd_send.at[r], fwd_recv.at[r],
            device_id=sibling, device_id_type=MESH).wait_recv()
        outer_block(where)

    for k in range(1, shards):
        part_copy(k).wait_send()
    z_copy.wait_send()

    @pl.loop(1, PLANE)
    def _(r):
        sib_copy(r).wait_send()
        plane_copy(r).wait_send()
        all_copy(r).wait_send()
        fwd_copy(r).wait_send()

    sib_copy(0).wait_send()
    fwd_copy(0).wait_send()


def write_out(*refs):
    sources, targets, sems = refs[:4], refs[4:8], refs[8]
    copies = [pltpu.make_async_copy(s, t, sems.at[i]) for i, (s, t) in enumerate(zip(sources, targets))]
    for copy in copies:
        copy.start()
    for copy in copies:
        copy.wait()


def per_device(anchor, inner_drift, gradient, first_moment, second_moment, outer_momentum):
    rows, lanes = anchor.shape
    shards = lax.axis_size("fsdp")
    islands = float(lax.axis_size("island"))
    limit = math.sqrt(shards * rows * lanes)
    step = rows // 2 // PLANE
    f32 = jnp.float32
    whole = pltpu.VMEM((rows, lanes), f32)
    blocks = pltpu.VMEM((PLANE, step, lanes), f32)
    block = pltpu.VMEM((step, lanes), f32)
    dma = pltpu.SemaphoreType.DMA
    hbm = pl.BlockSpec(memory_space=pltpu.HBM)
    vmem = pl.BlockSpec(memory_space=pltpu.VMEM)
    results = pl.pallas_call(
        functools.partial(kernel, shards, islands, limit),
        out_shape=[pltpu.VMEM((rows, lanes), f32)] * 4,
        in_specs=[hbm] * 6,
        out_specs=[vmem] * 4,
        scratch_shapes=[
            whole, whole, pltpu.VMEM((rows, lanes), jnp.bfloat16), whole, whole, whole,
            pltpu.VMEM((8, lanes), f32), pltpu.VMEM((shards, 8, lanes), f32),
            blocks, blocks, blocks, blocks, blocks, block, block, whole,
            dma((6,)), dma((shards,)), dma((shards,)), dma((PLANE,)), dma((PLANE,)),
            dma((PLANE,)), dma((PLANE,)), dma, dma, dma((PLANE,)), dma((PLANE,)), dma((PLANE,)), dma((PLANE,)),
        ],
        compiler_params=pltpu.CompilerParams(
            collective_id=0, has_side_effects=True, vmem_limit_bytes=60 * 1024 * 1024),
        cost_estimate=pl.CostEstimate(flops=40 * rows * lanes, bytes_accessed=40 * rows * lanes, transcendentals=0),
    )(anchor, inner_drift[0], gradient[0], first_moment[0], second_moment[0], outer_momentum)
    nf, ns, na, nm = pl.pallas_call(
        write_out,
        out_shape=[jax.ShapeDtypeStruct((rows, lanes), f32)] * 4,
        in_specs=[pl.BlockSpec(memory_space=pl.ANY)] * 4,
        out_specs=[hbm] * 4,
        scratch_shapes=[dma((4,))],
        compiler_params=pltpu.CompilerParams(vmem_limit_bytes=1024 * 1024),
        cost_estimate=pl.CostEstimate(flops=0, bytes_accessed=16 * rows * lanes, transcendentals=0),
    )(*results)
    return (nf[None], ns[None], na, nm)


def solution(mesh):
    return jax.shard_map(
        per_device,
        mesh=mesh,
        in_specs=(
            P("fsdp", None),
            P("island", "fsdp", None),
            P("island", "fsdp", None),
            P("island", "fsdp", None),
            P("island", "fsdp", None),
            P("fsdp", None),
        ),
        out_specs=(
            P("island", "fsdp", None),
            P("island", "fsdp", None),
            P("fsdp", None),
            P("fsdp", None),
        ),
        check_vma=False,
    )
```

time: 1130 us -> 47.8 us (0.04)
  waiting for transfers between devices: 1070 us -> 0 us
  Pallas kernels: 0 us -> 47 us
  blocking collectives: 34 us -> 0 us
  between operations: 14.8 us -> 0.64 us
    psum x1 -> x0, waiting for transfers between devices: 1070 us -> none  [per_device(): summed = lax.psum(pseudo, 'island')]
    pallas_call x0 -> x2, Pallas kernels: none -> 47 us  [the longest x1 45.7 us: per_device(): pl.pallas_call(functools.partial(kernel, shards, islands, limit), out_sha...]
    psum x1 -> x0, blocking collectives: 34 us -> none  [per_device(): squares = lax.psum(jnp.sum(wide * wide), 'fsdp')]
  transfers between devices with their start and end apart: 1 -> 0, of which waited for: 1 -> 0; matrix products, arithmetic and copies ran while one was open for 0% -> 0% of each run, Pallas kernels for 0% -> 0%
where the time goes in v1:
time: 47.8 us; the launch traced here: 47.7 us
  Pallas kernels  47 us (98%)
  between operations  0.64 us (1%)
    pallas_call x1, Pallas kernels, per_device(): pl.pallas_call(functools.partial(kernel, shards, islands, limit), out_sha...  45.7 us
    pallas_call x1, Pallas kernels, per_device(): pl.pallas_call(write_out, out_shape=[jax.ShapeDtypeStruct((rows, lanes),...  1.35 us

profile of v1, /device:TPU:1, one launch (start us, length us, event | category | flops | bytes accessed | tf_op | source)
XLA Modules:
  0.0 47.7 jit_solution(4653779035978179428)
XLA Ops:
  0.6 45.7 %shard_map.93 = (f32[1024,128]{1,0:T(8,128)S(1)}, f32[1024,128]{1,0:T(8,128)S(1)}, f32[1024,128]{1,0:T(8,128)S(1)}, f32[1024,128]{1,0:T(8,128)S(1)}) custom-call(f32[1024,128]{1,0:T(8,128)} %anchor_hbm.1, f32[1024,128]{1,0:T(8,128)} %bitcast.6, bf16[1024,128]{1,0:T(8,128)(2,1)} %bitcast.9, f32[1024,128]{1,0:T(8,128)} %bitcast.7, f32[1024,128]{1,0:T(8,128)} %bitcast.8, ...), custom_call_target="tpu_custom_call" | custom-call | flops 5242880 | bytes 5242880 | tf_op jit(solution)/shard_map/pallas_call | solution.py:241
  46.3 1.3 %shard_map.94 = (f32[1024,128]{1,0:T(8,128)}, f32[1024,128]{1,0:T(8,128)}, f32[1024,128]{1,0:T(8,128)}, f32[1024,128]{1,0:T(8,128)}) custom-call(f32[1024,128]{1,0:T(8,128)S(1)} %get-tuple-element.12.refs_0_, f32[1024,128]{1,0:T(8,128)S(1)} %get-tuple-element.13.refs_1_, f32[1024,128]{1,0:T(8,128)S(1)} %get-tuple-element.14.refs_2_, ...), custom_call_target="tpu_custom_call" | custom-call | bytes 2097152 | tf_op jit(solution)/shard_map/pallas_call | solution.py:257
